TPU v7x, 32 devices: a whole 2x2x4 slice. The times are simulated.
32 devices in a mesh: dp: 4 (over x, core), fsdp: 4 (over z), sp: 2 (over y).
Axes of the slice: x: 2, y: 2, z: 4, core: 2. Of those that a mesh axis runs over, the one named last changes fastest.
Arguments:
- query_raw: bfloat16 [4, 1024, 5120], P('dp', ('fsdp', 'sp')), may hold values from -35 to 35
- query_tangent: bfloat16 [4, 1024, 5120], P('dp', ('fsdp', 'sp')), may hold values from -35 to 35
- key_raw: bfloat16 [4, 512, 5120], P('dp', 'fsdp', 'sp'), may hold values from -40 to 40
- value_text: bfloat16 [4, 512, 5120], P('dp', 'fsdp', 'sp'), may hold values from -6 to 6
- query_gain: float32 [5120], replicated, may hold values from 0.25 to 1.75
- key_gain: float32 [5120], P('sp'), may hold values from 0.25 to 1.75
Outputs:
- attn_tangent: bfloat16 [4, 1024, 5120], P('dp', ('fsdp', 'sp'))
All inputs are finite; a program needn't handle non-finite values.
Results may differ from a plain program's by a relative error of at most 0.012.
The roundings to bfloat16 on the way count: a program that leaves them out, or rounds other values in their place, can miss the bound.
Values may be sent and summed in bfloat16 or wider, within the bound.
A program may use at most 64 MiB of HBM per device.

v0:
```python
import jax
import jax.numpy as jnp
from jax import lax
from jax.sharding import PartitionSpec as P

D = 5120
HD = 128


epsilon = 1e-06


def norm_tangent(source, tangent, gain):
    floats = source.astype(jnp.float32)
    moving = tangent.astype(jnp.float32)
    inverse = lax.rsqrt(jnp.mean(floats * floats, axis=-1, keepdims=True) + epsilon)
    projected = jnp.mean(floats * moving, axis=-1, keepdims=True)
    primal_rows = (floats * inverse * gain).astype(jnp.bfloat16)
    tangent_rows = (gain * inverse * (moving - floats * inverse * inverse * projected)).astype(
        jnp.bfloat16
    )
    return (primal_rows, tangent_rows)


def choose_group(head_count, row_count):
    chosen = 1
    for candidate in range(1, head_count + 1):
        if head_count % candidate == 0 and candidate * row_count <= 1024:
            chosen = candidate
    return chosen


def split_heads(rows, group_count, per_group):
    row_count = rows.shape[0]
    return rows.reshape(row_count, group_count, per_group, HD).transpose(1, 2, 0, 3)


def attend_group(entries):
    queries, key_heads, value_heads = entries
    scale = HD ** (-0.5)
    paired = (
        jnp.einsum("shqe,hke->shqk", queries, key_heads, preferred_element_type=jnp.float32) * scale
    )
    scores = paired[0]
    slopes = paired[1]
    top = jnp.max(scores, axis=-1, keepdims=True)
    weights = jnp.exp(scores - top)
    total = jnp.sum(weights, axis=-1, keepdims=True)
    probs = weights / total
    tilted = probs * slopes
    slope_mean = jnp.sum(tilted, axis=-1)
    stacked = jnp.stack([probs, tilted])
    products = jnp.einsum(
        "shqk,hke->shqe", stacked, value_heads.astype(jnp.float32), precision=lax.Precision.HIGHEST
    )
    return products[1] - slope_mean[..., None] * products[0]


def attend_all(query_rows, tangent_rows, key_rows, value_rows):
    row_count, feature_count = query_rows.shape
    head_count = feature_count // HD
    per_group = choose_group(head_count, row_count)
    group_count = head_count // per_group
    queries = jnp.stack(
        [
            split_heads(query_rows, group_count, per_group),
            split_heads(tangent_rows, group_count, per_group),
        ],
        axis=1,
    )
    key_heads = split_heads(key_rows, group_count, per_group)
    value_heads = split_heads(value_rows, group_count, per_group)
    result = lax.map(attend_group, (queries, key_heads, value_heads))
    return result.transpose(2, 0, 1, 3).reshape(row_count, feature_count).astype(jnp.bfloat16)


def shards(query_raw, query_tangent, key_raw, value_text, query_gain, key_gain):
    query_rows, tangent_rows = norm_tangent(query_raw[0], query_tangent[0], query_gain)
    key_floats = key_raw.astype(jnp.float32)
    square_sums = lax.psum(jnp.sum(key_floats * key_floats, axis=-1), "sp")
    key_inverse = lax.rsqrt(square_sums / D + epsilon)
    key_rows = (key_floats * key_inverse[..., None] * key_gain).astype(jnp.bfloat16)
    wide_keys, wide_values = (
        lax.all_gather(key_rows, "sp", axis=2, tiled=True),
        lax.all_gather(value_text, "sp", axis=2, tiled=True),
    )
    full_keys, full_values = (
        lax.all_gather(wide_keys, "fsdp", axis=1, tiled=True),
        lax.all_gather(wide_values, "fsdp", axis=1, tiled=True),
    )
    result = attend_all(query_rows, tangent_rows, full_keys[0], full_values[0])[None]
    return result


def solution(mesh):
    return jax.shard_map(
        shards,
        mesh=mesh,
        in_specs=(
            P("dp", ("fsdp", "sp"), None),
            P("dp", ("fsdp", "sp"), None),
            P("dp", "fsdp", "sp"),
            P("dp", "fsdp", "sp"),
            P(),
            P("sp"),
        ),
        out_specs=P("dp", ("fsdp", "sp"), None),
        check_vma=False,
    )
```

profile of v0, /device:TPU:0, one launch (start us, length us, event | category | flops | bytes accessed | tf_op | source)
XLA Modules:
  0.0 306.7 jit_solution(16985116237881885398)
XLA Ops:
  7.3 1.4 copy.17
  9.1 5.9 %psum.7 = f32[1,128]{1,0:T(1,128)S(1)} all-reduce(f32[1,128]{1,0:T(1,128)S(1)} %bitcast.97), channel_id=1, replica_groups=mesh['dp'=4,'fsdp'=4,'sp'=2] {'sp'}, use_global_device_ids=true, to_apply=%region_3.0 | all-reduce | flops 128 | bytes 1024 | tf_op jit(solution)/shard_map/psum | solution.py:80
  14.9 1.2 fusion.21
  16.3 19.6 %all-gather.5.cloned.1.call-done = bf16[1,128,5120]{2,1,0:T(8,128)(2,1)} async-done(((bf16[1,128,2560]{2,1,0:T(8,128)(2,1)}), bf16[1,128,5120]{2,1,0:T(8,128)(2,1)}) %all-gather.5.cloned.1.call-update) | async-done | bytes 1310736 | tf_op jit(solution)/shard_map/all_gather | solution.py:85
  36.0 25.8 %all-gather.9.cloned.1.call-done = bf16[1,128,5120]{1,2,0:T(8,128)(2,1)} async-done(((bf16[1,128,2560]{1,2,0:T(8,128)(2,1)}), bf16[1,128,5120]{1,2,0:T(8,128)(2,1)}) %all-gather.9.cloned.1.call-update) | async-done | bytes 1310736 | tf_op jit(solution)/shard_map/all_gather | solution.py:84
  61.8 0.8 copy.18
  62.6 1.8 copy.19
  64.3 0.9 multiply_reduce_fusion.1
  65.2 0.9 fusion.22
  66.1 0.9 fusion.23
  67.0 1.7 pad_maximum_fusion.1
  68.7 92.7 %all-gather.7.cloned.1.call-done = bf16[1,512,5120]{2,1,0:T(8,128)(2,1)} async-done(((bf16[1,128,5120]{2,1,0:T(8,128)(2,1)}), bf16[1,512,5120]{2,1,0:T(8,128)(2,1)}) %all-gather.7.cloned.1.call-update) | async-done | bytes 5242896 | tf_op jit(solution)/shard_map/all_gather | solution.py:89
  161.4 8.0 %copy.16 = bf16[1,512,5120]{1,2,0:T(8,128)(2,1)} copy(bf16[1,512,5120]{2,1,0:T(8,128)(2,1)} %all-gather.7.cloned.1.call-done) | data formatting | bytes 10485760 | tf_op jit(solution)/shard_map/all_gather | solution.py:89
  169.4 89.6 %all-gather.11.cloned.1.call-done = bf16[1,512,5120]{1,2,0:T(8,128)(2,1)} async-done(((bf16[1,128,5120]{1,2,0:T(8,128)(2,1)}), bf16[1,512,5120]{1,2,0:T(8,128)(2,1)}) %all-gather.11.cloned.1.call-update) | async-done | bytes 5242896 | tf_op jit(solution)/shard_map/all_gather | solution.py:88
  258.9 38.5 %while.10 = (s32[]{:T(128)}, bf16[5,8,128,128]{2,3,0,1:T(8,128)(2,1)S(1)}, bf16[5,8,512,128]{2,3,1,0:T(8,128)(2,1)}, bf16[5,8,512,128]{2,3,1,0:T(8,128)(2,1)}, bf16[5,2,8,128,128]{3,4,2,0,1:T(8,128)(2,1)}, /*index=5*/s32[]{:T(128)}) while((s32[]{:T(128)}, bf16[5,8,128,128]{2,3,0,1:T(8,128)(2,1)S(1)}, bf16[5,8,512,128]{2,3,1,0:T(8,128)(2,1)}, ...), condition=%wide.region_8.9_spmd, body=%wide.region_4.8_spmd.sunk | while | flops 1886647296 | bytes 32543820 | solution.py:73
  258.9 1.1 constant_dynamic-slice_fusion.2
  260.3 2.0 multiply_bitcast_fusion.2
  263.6 2.9 fusion.38
  266.6 1.1 constant_dynamic-slice_fusion.2
  268.0 2.0 multiply_bitcast_fusion.2
  271.3 2.9 fusion.38
  274.3 1.1 constant_dynamic-slice_fusion.2
  275.7 2.0 multiply_bitcast_fusion.2
  279.0 2.9 fusion.38
  282.0 1.1 constant_dynamic-slice_fusion.2
  283.4 2.0 multiply_bitcast_fusion.2
  286.7 2.9 fusion.38
  289.7 1.1 constant_dynamic-slice_fusion.2
  291.1 2.0 multiply_bitcast_fusion.2
  294.4 2.9 fusion.38
  297.4 1.3 copy.22
  298.7 1.4 convert_element_type.64
  (50 shorter events, 9.6 us)
Async XLA Ops:
  6.5 8.4 %copy-start.3 = (f32[2560]{0:T(1024)S(1)}, f32[2560]{0:T(1024)}, u32[]{:S(2)}) copy-start(f32[2560]{0:T(1024)} %param.13) | copy-start | bytes 30724
  6.5 29.4 %all-gather.5.cloned.1.call-start = ((), (), s32[]{:S(2)}) async-start(), calls=%async_computation | async-start | bytes 1966080 | tf_op jit(solution)/shard_map/all_gather | solution.py:85
  7.3 54.5 %all-gather.9.cloned.1.call-start = ((), (), s32[]{:S(2)}) async-start(), calls=%async_computation.2 | async-start | bytes 1966080 | tf_op jit(solution)/shard_map/all_gather | solution.py:84
  16.2 45.6 %copy-start = (bf16[1,128,5120]{2,1,0:T(8,128)(2,1)S(1)}, bf16[1,128,5120]{2,1,0:T(8,128)(2,1)}, u32[]{:S(2)}) copy-start(bf16[1,128,5120]{2,1,0:T(8,128)(2,1)} %param.8) | copy-start | bytes 3932164
  16.2 145.2 %all-gather.7.cloned.1.call-start = ((), (), s32[]{:S(2)}) async-start(), calls=%async_computation.1 | async-start | bytes 6553600 | tf_op jit(solution)/shard_map/all_gather | solution.py:89
  35.9 223.0 %all-gather.11.cloned.1.call-start = ((), (), s32[]{:S(2)}) async-start(), calls=%async_computation.3 | async-start | bytes 6553600 | tf_op jit(solution)/shard_map/all_gather | solution.py:88
  62.6 2.7 copy-start.2
  68.7 190.2 %copy-start.1 = (bf16[5,8,128,128]{2,3,0,1:T(8,128)(2,1)S(1)}, bf16[5,8,128,128]{2,3,0,1:T(8,128)(2,1)}, u32[]{:S(2)}) copy-start(bf16[5,8,128,128]{2,3,0,1:T(8,128)(2,1)} %custom-call) | copy-start | bytes 3932164
Sparse Core Ops, SparseCore 0:
  8.9 26.9 all-gather.4
  37.4 24.2 all-gather.8
  63.3 98.0 all-gather.6
  162.8 96.0 all-gather.10
where the time goes:
time: 308 us; the launch traced here: 307 us
  waiting for transfers between devices  228 us (74%)
  matrix products  24.4 us (8%)
  local copies, waits for them, and re-layouts  21.5 us (7%)
  between operations  13.2 us (4%)
  other arithmetic  12.9 us (4%)
  blocking collectives  5.86 us (2%)
    all_gather x1, waiting for transfers between devices, shards(): lax.all_gather(wide_values, 'fsdp', axis=1, tiled=True)  92.7 us
    all_gather x1, waiting for transfers between devices, shards(): lax.all_gather(wide_keys, 'fsdp', axis=1, tiled=True)  89.6 us
    all_gather x1, waiting for transfers between devices, shards(): lax.all_gather(key_rows, 'sp', axis=2, tiled=True)  25.8 us
    all_gather x1, waiting for transfers between devices, shards(): lax.all_gather(value_text, 'sp', axis=2, tiled=True)  19.6 us
    dot_general x5, matrix products, attend_group(): jnp.einsum('shqk,hke->shqe', stacked, value_heads.astype(jnp.float32), pr...  14.4 us
    dot_general x5, matrix products, attend_group(): jnp.einsum('shqe,hke->shqk', queries, key_heads, preferred_element_type=j...  9.94 us
    all_gather x1, local copies, waits for them, and re-layouts, shards(): lax.all_gather(wide_values, 'fsdp', axis=1, tiled=True)  7.97 us
    dynamic_slice x10, local copies, waits for them, and re-layouts, attend_all(): result = lax.map(attend_group, (queries, key_heads, value_heads))  6.82 us
  transfers between devices with their start and end apart: 4, of which 4 were waited for; matrix products, arithmetic and copies ran while one was open for 6% of the time, Pallas kernels for 0%

commit v1 on v0

v1 whole, which is shorter than its diff:
```python
import functools

import jax
import jax.numpy as jnp
from jax import lax
from jax.experimental import pallas as pl
from jax.experimental.pallas import tpu as pltpu
from jax.sharding import PartitionSpec as P

HD = 128
epsilon = 1e-06
MESH = pl.DeviceIdType.MESH


def choose_groups(heads):
    for count in (5, 4, 3, 2):
        if heads % count == 0:
            return count
    return 1


def kernel(
    n, s, groups,
    qr_ref, qt_ref, kr_ref, v_ref, qg_ref, kg_ref, out_ref,
    kbuf, vbuf, qsend, qbuf, obuf, ssbuf,
    vload_sem, kv_send, kv_recv, q_send, q_recv, ss_send, ss_recv, o_send, o_recv, own_sem,
):
    t, d = qr_ref.shape
    c, fl = kr_ref.shape
    fg = fl // groups
    per_group = fg // HD
    r = lax.axis_index("fsdp")
    p = lax.axis_index("sp")
    bufs = (kbuf, vbuf)

    def peer(dj):
        return lax.rem(p + dj, s)

    def origin(dj):
        return lax.rem(p + s - dj, s)

    def vload(g):
        columns = pl.ds(g * fg, fg)
        return pltpu.make_async_copy(v_ref.at[:, columns], vbuf.at[g, r], vload_sem.at[g])

    def piece(kind, g, src, way):
        target = r - 1 if way == 0 else r + 1
        buf = bufs[kind]
        return pltpu.make_async_remote_copy(
            src_ref=buf.at[g, src],
            dst_ref=buf.at[g, src],
            send_sem=kv_send.at[kind, way, g, src],
            recv_sem=kv_recv.at[kind, g, src],
            device_id={"fsdp": target},
            device_id_type=MESH,
        )

    def sums(dj):
        return pltpu.make_async_remote_copy(
            src_ref=ssbuf.at[0],
            dst_ref=ssbuf.at[dj],
            send_sem=ss_send.at[dj - 1],
            recv_sem=ss_recv.at[dj - 1],
            device_id={"sp": peer(dj)},
            device_id_type=MESH,
        )

    def queries(g, dj):
        return pltpu.make_async_remote_copy(
            src_ref=qsend.at[dj - 1, g],
            dst_ref=qbuf.at[g, dj],
            send_sem=q_send.at[g, dj - 1],
            recv_sem=q_recv.at[g, dj - 1],
            device_id={"sp": peer(dj)},
            device_id_type=MESH,
        )

    def output(g, dj):
        columns = pl.ds(pl.multiple_of(p * fl + g * fg, HD), fg)
        return pltpu.make_async_remote_copy(
            src_ref=obuf.at[g, dj],
            dst_ref=out_ref.at[:, columns],
            send_sem=o_send.at[g, dj - 1],
            recv_sem=o_recv.at[g, dj - 1],
            device_id={"sp": origin(dj)},
            device_id_type=MESH,
        )

    def own_output(g):
        columns = pl.ds(pl.multiple_of(p * fl + g * fg, HD), fg)
        return pltpu.make_async_copy(obuf.at[g, 0], out_ref.at[:, columns], own_sem.at[g])

    has_left = r > 0
    has_right = r < n - 1

    barrier = pltpu.get_barrier_semaphore()
    for dj in range(1, s):
        pl.semaphore_signal(barrier, inc=1, device_id={"sp": peer(dj)}, device_id_type=MESH)

    @pl.when(has_left)
    def _():
        pl.semaphore_signal(barrier, inc=1, device_id={"fsdp": r - 1}, device_id_type=MESH)

    @pl.when(has_right)
    def _():
        pl.semaphore_signal(barrier, inc=1, device_id={"fsdp": r + 1}, device_id_type=MESH)

    for g in range(groups):
        vload(g).start()

    acc = jnp.zeros((c, HD), jnp.float32)
    for i in range(fl // HD):
        x = kr_ref[:, i * HD:(i + 1) * HD].astype(jnp.float32)
        acc = acc + x * x
    ssbuf[0] = jnp.broadcast_to(jnp.sum(acc, axis=-1, keepdims=True), (c, HD))

    pl.semaphore_wait(barrier, s - 1 + has_left.astype(jnp.int32) + has_right.astype(jnp.int32))

    for dj in range(1, s):
        sums(dj).start()
    for g in range(groups):
        vload(g).wait()

    def send_own(kind, g):
        @pl.when(has_left)
        def _():
            piece(kind, g, r, 0).start()

        @pl.when(has_right)
        def _():
            piece(kind, g, r, 1).start()

    ahead = min(2, groups)
    for g in range(ahead):
        send_own(1, g)

    for dj in range(1, s):
        sums(dj).wait_recv()
    total = ssbuf[0]
    for dj in range(1, s):
        total = total + ssbuf[dj]
    key_inverse = lax.rsqrt(total * (1.0 / d) + epsilon)
    for g in range(groups):
        for i in range(per_group):
            lo = g * fg + i * HD
            x = kr_ref[:, lo:lo + HD].astype(jnp.float32)
            kbuf[g, r, :, i * HD:(i + 1) * HD] = (
                x * key_inverse * kg_ref[:, lo:lo + HD]
            ).astype(jnp.bfloat16)
        if g < ahead:
            send_own(0, g)

    square = jnp.zeros((t, HD), jnp.float32)
    cross = jnp.zeros((t, HD), jnp.float32)
    for i in range(d // HD):
        x = qr_ref[:, i * HD:(i + 1) * HD].astype(jnp.float32)
        y = qt_ref[:, i * HD:(i + 1) * HD].astype(jnp.float32)
        square = square + x * x
        cross = cross + x * y
    inverse = lax.rsqrt(jnp.sum(square, axis=-1, keepdims=True) * (1.0 / d) + epsilon)
    along = jnp.sum(cross, axis=-1, keepdims=True) * (1.0 / d)
    bend = inverse * inverse * along
    inverse = jnp.broadcast_to(inverse, (t, HD))
    bend = jnp.broadcast_to(bend, (t, HD))

    def norm_group(g, carry):
        for dj in [*range(1, s), 0]:
            j = peer(dj)
            for i in range(per_group):
                columns = pl.ds(pl.multiple_of(j * fl + g * fg + i * HD, HD), HD)
                x = qr_ref[:, columns].astype(jnp.float32)
                y = qt_ref[:, columns].astype(jnp.float32)
                gain = qg_ref[:, columns]
                primal = (x * inverse * gain).astype(jnp.bfloat16)
                tangent = (gain * inverse * (y - x * bend)).astype(jnp.bfloat16)
                if dj == 0:
                    qbuf[g, 0, 0, :, i * HD:(i + 1) * HD] = primal
                    qbuf[g, 0, 1, :, i * HD:(i + 1) * HD] = tangent
                else:
                    qsend[dj - 1, g, 0, :, i * HD:(i + 1) * HD] = primal
                    qsend[dj - 1, g, 1, :, i * HD:(i + 1) * HD] = tangent
            if dj > 0:
                queries(g, dj).start()
        return carry

    lax.fori_loop(0, groups, norm_group, 0)

    scale = HD ** (-0.5)

    def attend(g):
        for i in range(per_group):
            columns = slice(i * HD, (i + 1) * HD)
            keys = kbuf[g, :, :, columns].reshape(n * c, HD)
            values = vbuf[g, :, :, columns].reshape(n * c, HD)
            for dj in range(s):
                rows = qbuf[g, dj, :, :, columns].reshape(2 * t, HD)
                paired = lax.dot_general(
                    rows, keys, (((1,), (1,)), ((), ())), preferred_element_type=jnp.float32
                )
                scores, slopes = paired[:t], paired[t:]
                top = jnp.max(scores, axis=-1, keepdims=True)
                weights = jnp.exp((scores - top) * scale)
                whole = jnp.sum(weights, axis=-1, keepdims=True)
                mean = jnp.sum(weights * slopes, axis=-1, keepdims=True) / whole
                tilted = weights * (slopes - mean)
                high = tilted.astype(jnp.bfloat16)
                low = (tilted - high.astype(jnp.float32)).astype(jnp.bfloat16)
                result = jnp.dot(high, values, preferred_element_type=jnp.float32)
                result = result + jnp.dot(low, values, preferred_element_type=jnp.float32)
                obuf[g, dj, :, columns] = (result * (scale / whole)).astype(jnp.bfloat16)

    def step(g, carry):
        @pl.when(g + ahead < groups)
        def _():
            send_own(1, g + ahead)
            send_own(0, g + ahead)

        for h in range(1, n):
            for kind in (1, 0):
                @pl.when(r + h < n)
                def _():
                    piece(kind, g, r + h, 0).wait_recv()

                    @pl.when(has_left)
                    def _():
                        piece(kind, g, r + h, 0).start()

                @pl.when(r - h >= 0)
                def _():
                    piece(kind, g, r - h, 1).wait_recv()

                    @pl.when(has_right)
                    def _():
                        piece(kind, g, r - h, 1).start()

        for dj in range(1, s):
            queries(g, dj).wait_recv()
        attend(g)
        own_output(g).start()
        for dj in range(1, s):
            output(g, dj).start()
        return carry

    lax.fori_loop(0, groups, step, 0)

    for dj in range(1, s):
        sums(dj).wait_send()

    def finish(g, carry):
        for kind in (1, 0):
            for h in range(n):
                @pl.when(jnp.logical_and(r + h < n, has_left))
                def _():
                    piece(kind, g, r + h, 0).wait_send()

                @pl.when(jnp.logical_and(r - h >= 0, has_right))
                def _():
                    piece(kind, g, r - h, 1).wait_send()
        own_output(g).wait()
        for dj in range(1, s):
            queries(g, dj).wait_send()
            output(g, dj).wait_send()
            output(g, dj).wait_recv()
        return carry

    lax.fori_loop(0, groups, finish, 0)


def shards(n, s, query_raw, query_tangent, key_raw, value_text, query_gain, key_gain):
    _, t, d = query_raw.shape
    _, c, fl = key_raw.shape
    groups = choose_groups(fl // HD)
    fg = fl // groups
    peers = max(s - 1, 1)
    vmem = pl.BlockSpec(memory_space=pltpu.VMEM)
    anywhere = pl.BlockSpec(memory_space=pl.ANY)
    flops = 2 * 4 * s * t * n * c * fl
    moved = 2 * (3 * t * d + 2 * c * fl)
    result = pl.pallas_call(
        functools.partial(kernel, n, s, groups),
        out_shape=jax.ShapeDtypeStruct((t, d), jnp.bfloat16),
        in_specs=[vmem, vmem, vmem, anywhere, vmem, vmem],
        out_specs=anywhere,
        scratch_shapes=[
            pltpu.VMEM((groups, n, c, fg), jnp.bfloat16),
            pltpu.VMEM((groups, n, c, fg), jnp.bfloat16),
            pltpu.VMEM((peers, groups, 2, t, fg), jnp.bfloat16),
            pltpu.VMEM((groups, s, 2, t, fg), jnp.bfloat16),
            pltpu.VMEM((groups, s, t, fg), jnp.bfloat16),
            pltpu.VMEM((s, c, HD), jnp.float32),
            pltpu.SemaphoreType.DMA((groups,)),
            pltpu.SemaphoreType.DMA((2, 2, groups, n)),
            pltpu.SemaphoreType.DMA((2, groups, n)),
            pltpu.SemaphoreType.DMA((groups, peers)),
            pltpu.SemaphoreType.DMA((groups, peers)),
            pltpu.SemaphoreType.DMA((peers,)),
            pltpu.SemaphoreType.DMA((peers,)),
            pltpu.SemaphoreType.DMA((groups, peers)),
            pltpu.SemaphoreType.DMA((groups, peers)),
            pltpu.SemaphoreType.DMA((groups,)),
        ],
        compiler_params=pltpu.CompilerParams(
            collective_id=0, has_side_effects=True, vmem_limit_bytes=44 * 1024 * 1024
        ),
        cost_estimate=pl.CostEstimate(
            flops=flops, bytes_accessed=moved, transcendentals=s * t * n * c * (fl // HD)
        ),
    )(
        query_raw[0], query_tangent[0], key_raw[0], value_text[0],
        query_gain[None], key_gain[None],
    )
    return result[None]


def solution(mesh):
    n, s = mesh.shape["fsdp"], mesh.shape["sp"]
    return jax.shard_map(
        functools.partial(shards, n, s),
        mesh=mesh,
        in_specs=(
            P("dp", ("fsdp", "sp"), None),
            P("dp", ("fsdp", "sp"), None),
            P("dp", "fsdp", "sp"),
            P("dp", "fsdp", "sp"),
            P(),
            P("sp"),
        ),
        out_specs=P("dp", ("fsdp", "sp"), None),
        check_vma=False,
    )
```

time: 308 us -> 106 us (0.34)
  waiting for transfers between devices: 228 us -> 0 us
  Pallas kernels: 0 us -> 98.6 us
  matrix products: 24.4 us -> 0 us
  local copies, waits for them, and re-layouts: 21.5 us -> 7.3 us
  between operations: 13.2 us -> 0.02 us
  other arithmetic: 12.9 us -> 0 us
  blocking collectives: 5.86 us -> 0 us
    all_gather x4 -> x0, waiting for transfers between devices: 228 us -> none  [the longest x1 92.7 us: shards(): lax.all_gather(wide_values, 'fsdp', axis=1, tiled=True)]
    pallas_call x0 -> x1, Pallas kernels: none -> 98.6 us  [shards(): pl.pallas_call(functools.partial(kernel, n, s, groups), out_shape=jax.Sha...]
    dot_general x10 -> x0, matrix products: 24.4 us -> none  [the longest x5 14.4 us: attend_group(): jnp.einsum('shqk,hke->shqe', stacked, value_heads.astype(jnp.float32), pr...]
    all_gather x1 -> x0, local copies, waits for them, and re-layouts: 7.97 us -> none  [shards(): lax.all_gather(wide_values, 'fsdp', axis=1, tiled=True)]
    dynamic_slice x10 -> x0, local copies, waits for them, and re-layouts: 6.82 us -> none  [attend_all(): result = lax.map(attend_group, (queries, key_heads, value_heads))]
    psum x1 -> x0, blocking collectives: 5.86 us -> none  [shards(): square_sums = lax.psum(jnp.sum(key_floats * key_floats, axis=-1), 'sp')]
    reduce_sum x12 -> x0, other arithmetic: 4.79 us -> none  [the longest x5 2.11 us: attend_group(): slope_mean = jnp.sum(tilted, axis=-1)]
    another operation x3 -> x0, other arithmetic: 3.48 us -> none  [attend_all(): jnp.stack([split_heads(query_rows, group_count, per_group), split_heads(t...]
  transfers between devices with their start and end apart: 4 -> 0, of which waited for: 4 -> 0; matrix products, arithmetic and copies ran while one was open for 6% -> 0% of each run, Pallas kernels for 0% -> 0%
where the time goes in v1:
time: 106 us
  Pallas kernels  98.6 us (93%)
  local copies, waits for them, and re-layouts  7.3 us (7%)
    pallas_call x1, Pallas kernels, shards(): pl.pallas_call(functools.partial(kernel, n, s, groups), out_shape=jax.Sha...  98.6 us
    unnamed x11, local copies, waits for them, and re-layouts  6.59 us

profile of v1, /device:TPU:0, one launch (start us, length us, event | category | flops | bytes accessed | tf_op | source)
XLA Modules:
  0.0 105.9 jit_solution(17958419954078522367)
XLA Ops:
  0.0 0.7 broadcast_in_dim.10.kg_ref
  0.7 0.0 copy-start
  0.7 1.3 %copy-done = bf16[1,128,5120]{2,1,0:T(8,128)(2,1)S(1)} copy-done((bf16[1,128,5120]{2,1,0:T(8,128)(2,1)S(1)}, bf16[1,128,5120]{2,1,0:T(8,128)(2,1)}, u32[]{:S(2)}) %copy-start) | copy-done | bytes 1310744
  2.0 0.0 copy-start.1
  2.0 1.3 %copy-done.1 = bf16[1,128,5120]{2,1,0:T(8,128)(2,1)S(1)} copy-done((bf16[1,128,5120]{2,1,0:T(8,128)(2,1)S(1)}, bf16[1,128,5120]{2,1,0:T(8,128)(2,1)}, u32[]{:S(2)}) %copy-start.1) | copy-done | bytes 1310744
  3.3 0.0 copy-start.2
  3.4 1.1 %copy-done.2 = bf16[1,128,2560]{2,1,0:T(8,128)(2,1)S(1)} copy-done((bf16[1,128,2560]{2,1,0:T(8,128)(2,1)S(1)}, bf16[1,128,2560]{2,1,0:T(8,128)(2,1)}, u32[]{:S(2)}) %copy-start.2) | copy-done | bytes 655384
  4.4 0.0 copy-start.3
  4.4 1.1 %copy-done.3 = bf16[1,128,2560]{2,1,0:T(8,128)(2,1)S(1)} copy-done((bf16[1,128,2560]{2,1,0:T(8,128)(2,1)S(1)}, bf16[1,128,2560]{2,1,0:T(8,128)(2,1)}, u32[]{:S(2)}) %copy-start.3) | copy-done | bytes 655384
  5.5 0.0 copy-start.4
  5.5 0.7 copy-done.4
  6.3 98.6 %shard_map.64 = bf16[128,5120]{1,0:T(8,128)(2,1)S(1)} custom-call(bf16[128,5120]{1,0:T(8,128)(2,1)S(1)} %bitcast.7, bf16[128,5120]{1,0:T(8,128)(2,1)S(1)} %bitcast.8, bf16[128,2560]{1,0:T(8,128)(2,1)S(1)} %bitcast.9, bf16[128,2560]{1,0:T(8,128)(2,1)S(1)} %bitcast.10, f32[1,5120]{1,0:T(1,128)S(1)} %bitcast.11, f32[1,2560]{1,0:T(1,128)S(1)} %broadcast_in_dim.10.kg_ref), custom_call_target="tpu_custom_call" | custom-call | flops 2684354560 | bytes 5242880 | tf_op jit(solution)/shard_map/pallas_call | solution.py:279
  104.8 1.1 %copy.8 = bf16[1,128,5120]{2,1,0:T(8,128)(2,1)} copy(bf16[1,128,5120]{2,1,0:T(8,128)(2,1)S(1)} %bitcast.6) | data formatting | bytes 2621440
Async XLA Ops:
  0.7 1.3 %copy-start = (bf16[1,128,5120]{2,1,0:T(8,128)(2,1)S(1)}, bf16[1,128,5120]{2,1,0:T(8,128)(2,1)}, u32[]{:S(2)}) copy-start(bf16[1,128,5120]{2,1,0:T(8,128)(2,1)} %param.6) | copy-start | bytes 3932164
  2.0 1.3 %copy-start.1 = (bf16[1,128,5120]{2,1,0:T(8,128)(2,1)S(1)}, bf16[1,128,5120]{2,1,0:T(8,128)(2,1)}, u32[]{:S(2)}) copy-start(bf16[1,128,5120]{2,1,0:T(8,128)(2,1)} %param.7) | copy-start | bytes 3932164
  3.3 1.1 %copy-start.2 = (bf16[1,128,2560]{2,1,0:T(8,128)(2,1)S(1)}, bf16[1,128,2560]{2,1,0:T(8,128)(2,1)}, u32[]{:S(2)}) copy-start(bf16[1,128,2560]{2,1,0:T(8,128)(2,1)} %param.8) | copy-start | bytes 1966084
  4.4 1.1 %copy-start.3 = (bf16[1,128,2560]{2,1,0:T(8,128)(2,1)S(1)}, bf16[1,128,2560]{2,1,0:T(8,128)(2,1)}, u32[]{:S(2)}) copy-start(bf16[1,128,2560]{2,1,0:T(8,128)(2,1)} %param.9) | copy-start | bytes 1966084
  5.5 0.7 copy-start.4

commit v2 on v1

--- a/solution.py
+++ b/solution.py
@@ -13,7 +13,7 @@
 
 
 def choose_groups(heads):
-    for count in (5, 4, 3, 2):
+    for count in (10, 8, 6, 5, 4, 3, 2):
         if heads % count == 0:
             return count
     return 1
@@ -21,17 +21,21 @@
 
 def kernel(
     n, s, groups,
-    qr_ref, qt_ref, kr_ref, v_ref, qg_ref, kg_ref, out_ref,
-    kbuf, vbuf, qsend, qbuf, obuf, ssbuf,
-    vload_sem, kv_send, kv_recv, q_send, q_recv, ss_send, ss_recv, o_send, o_recv, own_sem,
+    qr_hbm, qt_hbm, kr_hbm, v_ref, qg_hbm, kg_hbm, out_ref,
+    qr_ref, qt_ref, kr_ref, qg_ref, kg_ref,
+    kbuf, vbuf, qsend, qbuf, xbuf, obuf, ybuf, ssbuf,
+    load_sem, vload_sem, kv_send, kv_recv, q_send, q_recv, x_send, x_recv,
+    ss_send, ss_recv, o_send, o_recv, y_send, own_sem,
 ):
     t, d = qr_ref.shape
+    inputs = ((kr_hbm, kr_ref), (kg_hbm, kg_ref), (qr_hbm, qr_ref), (qt_hbm, qt_ref), (qg_hbm, qg_ref))
     c, fl = kr_ref.shape
     fg = fl // groups
     per_group = fg // HD
     r = lax.axis_index("fsdp")
     p = lax.axis_index("sp")
     bufs = (kbuf, vbuf)
+    partner = jnp.where(r == 0, 1, jnp.where(r == 1, 0, jnp.where(r == n - 1, n - 2, n - 1)))
 
     def peer(dj):
         return lax.rem(p + dj, s)
@@ -75,13 +79,34 @@
             device_id_type=MESH,
         )
 
+    def lend(g, dj):
+        return pltpu.make_async_remote_copy(
+            src_ref=qbuf.at[g, dj],
+            dst_ref=xbuf.at[g // 2, dj],
+            send_sem=x_send.at[g // 2, dj],
+            recv_sem=x_recv.at[g // 2, dj],
+            device_id={"fsdp": partner},
+            device_id_type=MESH,
+        )
+
+    def give_back(g, dj):
+        columns = pl.ds(pl.multiple_of(p * fl + g * fg, HD), fg)
+        return pltpu.make_async_remote_copy(
+            src_ref=ybuf.at[g // 2, dj],
+            dst_ref=out_ref.at[:, columns],
+            send_sem=y_send.at[g // 2, dj],
+            recv_sem=o_recv.at[g, dj],
+            device_id={"fsdp": partner, "sp": origin(dj)},
+            device_id_type=MESH,
+        )
+
     def output(g, dj):
         columns = pl.ds(pl.multiple_of(p * fl + g * fg, HD), fg)
         return pltpu.make_async_remote_copy(
             src_ref=obuf.at[g, dj],
             dst_ref=out_ref.at[:, columns],
             send_sem=o_send.at[g, dj - 1],
-            recv_sem=o_recv.at[g, dj - 1],
+            recv_sem=o_recv.at[g, dj],
             device_id={"sp": origin(dj)},
             device_id_type=MESH,
         )
@@ -92,6 +117,21 @@
 
     has_left = r > 0
     has_right = r < n - 1
+    lending = n >= 4
+    is_end = jnp.logical_or(r == 0, r == n - 1) if lending else r < 0
+    is_helper = jnp.logical_or(r == 1, r == n - 2) if lending else r < 0
+
+    def lent(g):
+        return lax.rem(jnp.int32(g), 2) == 0
+
+    def goes_left(g):
+        return r > jnp.where(lent(g), 1, 0) if lending else has_left
+
+    def goes_right(g):
+        return r < jnp.where(lent(g), n - 2, n - 1) if lending else has_right
+
+    def receives(g):
+        return jnp.logical_not(jnp.logical_and(is_end, lent(g)))
 
     barrier = pltpu.get_barrier_semaphore()
     for dj in range(1, s):
@@ -105,8 +145,21 @@
     def _():
         pl.semaphore_signal(barrier, inc=1, device_id={"fsdp": r + 1}, device_id_type=MESH)
 
+    if s > 1:
+        @pl.when(is_end)
+        def _():
+            for dj in range(1, s):
+                pl.semaphore_signal(
+                    barrier, inc=1, device_id={"fsdp": partner, "sp": peer(dj)}, device_id_type=MESH
+                )
+
+    loads = [pltpu.make_async_copy(a, b, load_sem.at[i]) for i, (a, b) in enumerate(inputs)]
+    loads[0].start()
     for g in range(groups):
         vload(g).start()
+    for load in loads[1:]:
+        load.start()
+    loads[0].wait()
 
     acc = jnp.zeros((c, HD), jnp.float32)
     for i in range(fl // HD):
@@ -114,7 +167,13 @@
         acc = acc + x * x
     ssbuf[0] = jnp.broadcast_to(jnp.sum(acc, axis=-1, keepdims=True), (c, HD))
 
-    pl.semaphore_wait(barrier, s - 1 + has_left.astype(jnp.int32) + has_right.astype(jnp.int32))
+    pl.semaphore_wait(
+        barrier,
+        s - 1
+        + has_left.astype(jnp.int32)
+        + has_right.astype(jnp.int32)
+        + (s - 1) * is_helper.astype(jnp.int32),
+    )
 
     for dj in range(1, s):
         sums(dj).start()
@@ -122,15 +181,15 @@
         vload(g).wait()
 
     def send_own(kind, g):
-        @pl.when(has_left)
+        @pl.when(goes_left(g))
         def _():
             piece(kind, g, r, 0).start()
 
-        @pl.when(has_right)
+        @pl.when(goes_right(g))
         def _():
             piece(kind, g, r, 1).start()
 
-    ahead = min(2, groups)
+    ahead = min(4, groups)
     for g in range(ahead):
         send_own(1, g)
 
@@ -139,17 +198,20 @@
     total = ssbuf[0]
     for dj in range(1, s):
         total = total + ssbuf[dj]
+    loads[1].wait()
     key_inverse = lax.rsqrt(total * (1.0 / d) + epsilon)
     for g in range(groups):
         for i in range(per_group):
             lo = g * fg + i * HD
             x = kr_ref[:, lo:lo + HD].astype(jnp.float32)
             kbuf[g, r, :, i * HD:(i + 1) * HD] = (
-                x * key_inverse * kg_ref[:, lo:lo + HD]
+                x * key_inverse * kg_ref[lo:lo + HD].reshape(1, HD)
             ).astype(jnp.bfloat16)
         if g < ahead:
             send_own(0, g)
 
+    for load in loads[2:]:
+        load.wait()
     square = jnp.zeros((t, HD), jnp.float32)
     cross = jnp.zeros((t, HD), jnp.float32)
     for i in range(d // HD):
@@ -187,13 +249,13 @@
 
     scale = HD ** (-0.5)
 
-    def attend(g):
+    def attend(g, rows_ref, place, into_ref, where):
         for i in range(per_group):
             columns = slice(i * HD, (i + 1) * HD)
             keys = kbuf[g, :, :, columns].reshape(n * c, HD)
             values = vbuf[g, :, :, columns].reshape(n * c, HD)
             for dj in range(s):
-                rows = qbuf[g, dj, :, :, columns].reshape(2 * t, HD)
+                rows = rows_ref[place, dj, :, :, columns].reshape(2 * t, HD)
                 paired = lax.dot_general(
                     rows, keys, (((1,), (1,)), ((), ())), preferred_element_type=jnp.float32
                 )
@@ -207,41 +269,79 @@
                 low = (tilted - high.astype(jnp.float32)).astype(jnp.bfloat16)
                 result = jnp.dot(high, values, preferred_element_type=jnp.float32)
                 result = result + jnp.dot(low, values, preferred_element_type=jnp.float32)
-                obuf[g, dj, :, columns] = (result * (scale / whole)).astype(jnp.bfloat16)
-
-    def step(g, carry):
-        @pl.when(g + ahead < groups)
-        def _():
-            send_own(1, g + ahead)
-            send_own(0, g + ahead)
-
+                into_ref[where, dj, :, columns] = (result * (scale / whole)).astype(jnp.bfloat16)
+
+    def launch(g):
+        send_own(1, g)
+        send_own(0, g)
+
+    def lend_group(g):
+        @pl.when(jnp.logical_and(is_end, lent(g)))
+        def _():
+            for dj in range(s):
+                if dj > 0:
+                    queries(g, dj).wait_recv()
+                lend(g, dj).start()
+
+    def forward(g):
         for h in range(1, n):
             for kind in (1, 0):
-                @pl.when(r + h < n)
+                @pl.when(jnp.logical_and(r + h < n, receives(g)))
                 def _():
                     piece(kind, g, r + h, 0).wait_recv()
 
-                    @pl.when(has_left)
+                    @pl.when(goes_left(g))
                     def _():
                         piece(kind, g, r + h, 0).start()
 
-                @pl.when(r - h >= 0)
+                @pl.when(jnp.logical_and(r - h >= 0, receives(g)))
                 def _():
                     piece(kind, g, r - h, 1).wait_recv()
 
-                    @pl.when(has_right)
+                    @pl.when(goes_right(g))
                     def _():
                         piece(kind, g, r - h, 1).start()
 
-        for dj in range(1, s):
-            queries(g, dj).wait_recv()
-        attend(g)
-        own_output(g).start()
-        for dj in range(1, s):
-            output(g, dj).start()
+    def work(g):
+        @pl.when(receives(g))
+        def _():
+            for dj in range(1, s):
+                queries(g, dj).wait_recv()
+            attend(g, qbuf, g, obuf, g)
+            own_output(g).start()
+            for dj in range(1, s):
+                output(g, dj).start()
+
+        @pl.when(jnp.logical_and(is_helper, lent(g)))
+        def _():
+            for dj in range(s):
+                lend(g, dj).wait_recv()
+            attend(g, xbuf, g // 2, ybuf, g // 2)
+            for dj in range(s):
+                give_back(g, dj).start()
+
+    for g in range(ahead):
+        lend_group(g)
+
+    lead = 1
+
+    def step(i, carry):
+        @pl.when(i + ahead < groups)
+        def _():
+            launch(i + ahead)
+            lend_group(i + ahead)
+
+        @pl.when(i < groups)
+        def _():
+            forward(i)
+
+        @pl.when(i >= lead)
+        def _():
+            work(i - lead)
+
         return carry
 
-    lax.fori_loop(0, groups, step, 0)
+    lax.fori_loop(0, groups + lead, step, 0)
 
     for dj in range(1, s):
         sums(dj).wait_send()
@@ -249,18 +349,36 @@
     def finish(g, carry):
         for kind in (1, 0):
             for h in range(n):
-                @pl.when(jnp.logical_and(r + h < n, has_left))
+                @pl.when(jnp.logical_and(r + h < n, goes_left(g)) if h == 0 else
+                         jnp.logical_and(jnp.logical_and(r + h < n, goes_left(g)), receives(g)))
                 def _():
                     piece(kind, g, r + h, 0).wait_send()
 
-                @pl.when(jnp.logical_and(r - h >= 0, has_right))
+                @pl.when(jnp.logical_and(r - h >= 0, goes_right(g)) if h == 0 else
+                         jnp.logical_and(jnp.logical_and(r - h >= 0, goes_right(g)), receives(g)))
                 def _():
                     piece(kind, g, r - h, 1).wait_send()
-        own_output(g).wait()
+
         for dj in range(1, s):
             queries(g, dj).wait_send()
-            output(g, dj).wait_send()
             output(g, dj).wait_recv()
+
+        @pl.when(receives(g))
+        def _():
+            own_output(g).wait()
+            for dj in range(1, s):
+                output(g, dj).wait_send()
+
+        @pl.when(jnp.logical_and(is_end, lent(g)))
+        def _():
+            for dj in range(s):
+                lend(g, dj).wait_send()
+            give_back(g, 0).wait_recv()
+
+        @pl.when(jnp.logical_and(is_helper, lent(g)))
+        def _():
+            for dj in range(s):
+                give_back(g, dj).wait_send()
         return carry
 
     lax.fori_loop(0, groups, finish, 0)
@@ -272,42 +390,53 @@
     groups = choose_groups(fl // HD)
     fg = fl // groups
     peers = max(s - 1, 1)
-    vmem = pl.BlockSpec(memory_space=pltpu.VMEM)
+    lots = (groups + 1) // 2
     anywhere = pl.BlockSpec(memory_space=pl.ANY)
     flops = 2 * 4 * s * t * n * c * fl
     moved = 2 * (3 * t * d + 2 * c * fl)
     result = pl.pallas_call(
         functools.partial(kernel, n, s, groups),
         out_shape=jax.ShapeDtypeStruct((t, d), jnp.bfloat16),
-        in_specs=[vmem, vmem, vmem, anywhere, vmem, vmem],
+        in_specs=[anywhere] * 6,
         out_specs=anywhere,
         scratch_shapes=[
+            pltpu.VMEM((t, d), jnp.bfloat16),
+            pltpu.VMEM((t, d), jnp.bfloat16),
+            pltpu.VMEM((c, fl), jnp.bfloat16),
+            pltpu.VMEM((1, d), jnp.float32),
+            pltpu.VMEM((fl,), jnp.float32),
             pltpu.VMEM((groups, n, c, fg), jnp.bfloat16),
             pltpu.VMEM((groups, n, c, fg), jnp.bfloat16),
             pltpu.VMEM((peers, groups, 2, t, fg), jnp.bfloat16),
             pltpu.VMEM((groups, s, 2, t, fg), jnp.bfloat16),
+            pltpu.VMEM((lots, s, 2, t, fg), jnp.bfloat16),
             pltpu.VMEM((groups, s, t, fg), jnp.bfloat16),
+            pltpu.VMEM((lots, s, t, fg), jnp.bfloat16),
             pltpu.VMEM((s, c, HD), jnp.float32),
+            pltpu.SemaphoreType.DMA((5,)),
             pltpu.SemaphoreType.DMA((groups,)),
             pltpu.SemaphoreType.DMA((2, 2, groups, n)),
             pltpu.SemaphoreType.DMA((2, groups, n)),
             pltpu.SemaphoreType.DMA((groups, peers)),
             pltpu.SemaphoreType.DMA((groups, peers)),
+            pltpu.SemaphoreType.DMA((lots, s)),
+            pltpu.SemaphoreType.DMA((lots, s)),
             pltpu.SemaphoreType.DMA((peers,)),
             pltpu.SemaphoreType.DMA((peers,)),
             pltpu.SemaphoreType.DMA((groups, peers)),
-            pltpu.SemaphoreType.DMA((groups, peers)),
+            pltpu.SemaphoreType.DMA((groups, s)),
+            pltpu.SemaphoreType.DMA((lots, s)),
             pltpu.SemaphoreType.DMA((groups,)),
         ],
         compiler_params=pltpu.CompilerParams(
-            collective_id=0, has_side_effects=True, vmem_limit_bytes=44 * 1024 * 1024
+            collective_id=0, has_side_effects=True, vmem_limit_bytes=60 * 1024 * 1024
         ),
         cost_estimate=pl.CostEstimate(
             flops=flops, bytes_accessed=moved, transcendentals=s * t * n * c * (fl // HD)
         ),
     )(
         query_raw[0], query_tangent[0], key_raw[0], value_text[0],
-        query_gain[None], key_gain[None],
+        query_gain[None], key_gain,
     )
     return result[None]
 

time: 106 us -> 105 us (level)
  local copies, waits for them, and re-layouts: 7.3 us -> 2.46 us
  Pallas kernels: 98.6 us -> 103 us
    unnamed x11 -> x1, local copies, waits for them, and re-layouts: 6.59 us -> 2.46 us
    pallas_call x1, Pallas kernels: 98.6 us -> 103 us  [shards(): pl.pallas_call(functools.partial(kernel, n, s, groups), out_shape=jax.Sha...]
where the time goes in v2:
time: 105 us
  Pallas kernels  103 us (98%)
  local copies, waits for them, and re-layouts  2.46 us (2%)
    pallas_call x1, Pallas kernels, shards(): pl.pallas_call(functools.partial(kernel, n, s, groups), out_shape=jax.Sha...  103 us
    unnamed x1, local copies, waits for them, and re-layouts  2.46 us

profile of v2, /device:TPU:0, one launch (start us, length us, event | category | flops | bytes accessed | tf_op | source)
XLA Modules:
  0.0 105.1 jit_solution(16007332893757406336)
XLA Ops:
  0.0 102.6 %shard_map.64 = bf16[128,5120]{1,0:T(8,128)(2,1)} custom-call(bf16[128,5120]{1,0:T(8,128)(2,1)} %bitcast.7, bf16[128,5120]{1,0:T(8,128)(2,1)} %bitcast.8, bf16[128,2560]{1,0:T(8,128)(2,1)} %bitcast.9, bf16[128,2560]{1,0:T(8,128)(2,1)} %bitcast.10, f32[1,5120]{1,0:T(1,128)} %bitcast.11, f32[2560]{0:T(1024)} %kg_hbm.1), custom_call_target="tpu_custom_call" | custom-call | flops 2684354560 | bytes 5242880 | tf_op jit(solution)/shard_map/pallas_call | solution.py:397
  102.6 2.5 %copy.8 = bf16[1,128,5120]{2,1,0:T(8,128)(2,1)} copy(bf16[1,128,5120]{2,1,0:T(8,128)(2,1)} %bitcast.6) | data formatting | bytes 2621440

commit v3 on v2

--- a/solution.py
+++ b/solution.py
@@ -8,6 +8,7 @@
 from jax.sharding import PartitionSpec as P
 
 HD = 128
+LOG2E = 1.4426950408889634
 epsilon = 1e-06
 MESH = pl.DeviceIdType.MESH
 
@@ -35,6 +36,10 @@
     r = lax.axis_index("fsdp")
     p = lax.axis_index("sp")
     bufs = (kbuf, vbuf)
+
+    def lot(g):
+        return g // 2
+
     partner = jnp.where(r == 0, 1, jnp.where(r == 1, 0, jnp.where(r == n - 1, n - 2, n - 1)))
 
     def peer(dj):
@@ -82,9 +87,9 @@
     def lend(g, dj):
         return pltpu.make_async_remote_copy(
             src_ref=qbuf.at[g, dj],
-            dst_ref=xbuf.at[g // 2, dj],
-            send_sem=x_send.at[g // 2, dj],
-            recv_sem=x_recv.at[g // 2, dj],
+            dst_ref=xbuf.at[lot(g), dj],
+            send_sem=x_send.at[lot(g), dj],
+            recv_sem=x_recv.at[lot(g), dj],
             device_id={"fsdp": partner},
             device_id_type=MESH,
         )
@@ -92,9 +97,9 @@
     def give_back(g, dj):
         columns = pl.ds(pl.multiple_of(p * fl + g * fg, HD), fg)
         return pltpu.make_async_remote_copy(
-            src_ref=ybuf.at[g // 2, dj],
+            src_ref=ybuf.at[lot(g), dj],
             dst_ref=out_ref.at[:, columns],
-            send_sem=y_send.at[g // 2, dj],
+            send_sem=y_send.at[lot(g), dj],
             recv_sem=o_recv.at[g, dj],
             device_id={"fsdp": partner, "sp": origin(dj)},
             device_id_type=MESH,
@@ -189,7 +194,7 @@
         def _():
             piece(kind, g, r, 1).start()
 
-    ahead = min(4, groups)
+    ahead = min(3, groups)
     for g in range(ahead):
         send_own(1, g)
 
@@ -249,27 +254,29 @@
 
     scale = HD ** (-0.5)
 
-    def attend(g, rows_ref, place, into_ref, where):
-        for i in range(per_group):
-            columns = slice(i * HD, (i + 1) * HD)
-            keys = kbuf[g, :, :, columns].reshape(n * c, HD)
-            values = vbuf[g, :, :, columns].reshape(n * c, HD)
-            for dj in range(s):
-                rows = rows_ref[place, dj, :, :, columns].reshape(2 * t, HD)
-                paired = lax.dot_general(
-                    rows, keys, (((1,), (1,)), ((), ())), preferred_element_type=jnp.float32
-                )
-                scores, slopes = paired[:t], paired[t:]
-                top = jnp.max(scores, axis=-1, keepdims=True)
-                weights = jnp.exp((scores - top) * scale)
-                whole = jnp.sum(weights, axis=-1, keepdims=True)
-                mean = jnp.sum(weights * slopes, axis=-1, keepdims=True) / whole
-                tilted = weights * (slopes - mean)
-                high = tilted.astype(jnp.bfloat16)
-                low = (tilted - high.astype(jnp.float32)).astype(jnp.bfloat16)
-                result = jnp.dot(high, values, preferred_element_type=jnp.float32)
-                result = result + jnp.dot(low, values, preferred_element_type=jnp.float32)
-                into_ref[where, dj, :, columns] = (result * (scale / whole)).astype(jnp.bfloat16)
+    def attend(g, i, rows_ref, place, into_ref, where):
+        columns = slice(i * HD, (i + 1) * HD)
+        keys = kbuf[g, :, :, columns].reshape(n * c, HD)
+        values = vbuf[g, :, :, columns].reshape(n * c, HD)
+        rows = rows_ref[place, :, :, :, columns].reshape(s * 2 * t, HD)
+        paired = lax.dot_general(
+            rows, keys, (((1,), (1,)), ((), ())), preferred_element_type=jnp.float32
+        ).reshape(s, 2, t, n * c)
+        tilts, factors = [], []
+        for dj in range(s):
+            scores, slopes = paired[dj, 0], paired[dj, 1]
+            top = jnp.max(scores, axis=-1, keepdims=True)
+            weights = jnp.exp2((scores - top) * (scale * LOG2E))
+            whole = jnp.sum(weights, axis=-1, keepdims=True)
+            mean = jnp.sum(weights * slopes, axis=-1, keepdims=True) / whole
+            tilts.append((weights * (slopes - mean)).astype(jnp.bfloat16))
+            factors.append(scale / whole)
+        tilted = jnp.concatenate(tilts, axis=0)
+        result = jnp.dot(tilted, values, preferred_element_type=jnp.float32)
+        for dj in range(s):
+            into_ref[where, dj, :, columns] = (
+                result[dj * t:(dj + 1) * t] * factors[dj]
+            ).astype(jnp.bfloat16)
 
     def launch(g):
         send_own(1, g)
@@ -283,47 +290,51 @@
                     queries(g, dj).wait_recv()
                 lend(g, dj).start()
 
-    def forward(g):
-        for h in range(1, n):
-            for kind in (1, 0):
-                @pl.when(jnp.logical_and(r + h < n, receives(g)))
-                def _():
-                    piece(kind, g, r + h, 0).wait_recv()
-
-                    @pl.when(goes_left(g))
-                    def _():
-                        piece(kind, g, r + h, 0).start()
-
-                @pl.when(jnp.logical_and(r - h >= 0, receives(g)))
-                def _():
-                    piece(kind, g, r - h, 1).wait_recv()
-
-                    @pl.when(goes_right(g))
-                    def _():
-                        piece(kind, g, r - h, 1).start()
-
-    def work(g):
+    def forward(g, h):
+        for kind in (1, 0):
+            @pl.when(jnp.logical_and(r + h < n, receives(g)))
+            def _():
+                piece(kind, g, r + h, 0).wait_recv()
+
+                @pl.when(goes_left(g))
+                def _():
+                    piece(kind, g, r + h, 0).start()
+
+            @pl.when(jnp.logical_and(r - h >= 0, receives(g)))
+            def _():
+                piece(kind, g, r - h, 1).wait_recv()
+
+                @pl.when(goes_right(g))
+                def _():
+                    piece(kind, g, r - h, 1).start()
+
+    def work(g, i):
         @pl.when(receives(g))
         def _():
-            for dj in range(1, s):
-                queries(g, dj).wait_recv()
-            attend(g, qbuf, g, obuf, g)
-            own_output(g).start()
-            for dj in range(1, s):
-                output(g, dj).start()
-
+            if i == 0:
+                for dj in range(1, s):
+                    queries(g, dj).wait_recv()
+            attend(g, i, qbuf, g, obuf, g)
+            if i == per_group - 1:
+                for dj in range(1, s):
+                    output(g, dj).start()
+                own_output(g).start()
+
+    def help_end(g, i):
         @pl.when(jnp.logical_and(is_helper, lent(g)))
         def _():
-            for dj in range(s):
-                lend(g, dj).wait_recv()
-            attend(g, xbuf, g // 2, ybuf, g // 2)
-            for dj in range(s):
-                give_back(g, dj).start()
+            if i == 0:
+                for dj in range(s):
+                    lend(g, dj).wait_recv()
+            attend(g, i, xbuf, lot(g), ybuf, lot(g))
+            if i == per_group - 1:
+                for dj in range(s):
+                    give_back(g, dj).start()
 
     for g in range(ahead):
         lend_group(g)
 
-    lead = 1
+    lead, lag = 1, 2
 
     def step(i, carry):
         @pl.when(i + ahead < groups)
@@ -331,17 +342,25 @@
             launch(i + ahead)
             lend_group(i + ahead)
 
-        @pl.when(i < groups)
-        def _():
-            forward(i)
-
-        @pl.when(i >= lead)
-        def _():
-            work(i - lead)
+        moves = list(range(1, n))
+        units = [(work, lead, k) for k in range(per_group)]
+        units += [(help_end, lag, k) for k in range(per_group)]
+        for k in range(max(len(moves), len(units))):
+            if k < len(moves):
+                @pl.when(i < groups)
+                def _():
+                    forward(i, moves[k])
+
+            if k < len(units):
+                unit, behind, part = units[k]
+
+                @pl.when(jnp.logical_and(i >= behind, i - behind < groups))
+                def _():
+                    unit(i - behind, part)
 
         return carry
 
-    lax.fori_loop(0, groups + lead, step, 0)
+    lax.fori_loop(0, max(groups + lead, groups - 1 + lag), step, 0)
 
     for dj in range(1, s):
         sums(dj).wait_send()
@@ -390,7 +409,7 @@
     groups = choose_groups(fl // HD)
     fg = fl // groups
     peers = max(s - 1, 1)
-    lots = (groups + 1) // 2
+    lots = groups // 2 + 1
     anywhere = pl.BlockSpec(memory_space=pl.ANY)
     flops = 2 * 4 * s * t * n * c * fl
     moved = 2 * (3 * t * d + 2 * c * fl)

time: 105 us -> 93.8 us (0.89)
  Pallas kernels: 103 us -> 91.2 us
    pallas_call x1, Pallas kernels: 103 us -> 91.2 us  [shards(): pl.pallas_call(functools.partial(kernel, n, s, groups), out_shape=jax.Sha...]
where the time goes in v3:
time: 93.8 us; the launch traced here: 93.7 us
  Pallas kernels  91.2 us (97%)
  local copies, waits for them, and re-layouts  2.46 us (3%)
    pallas_call x1, Pallas kernels, shards(): pl.pallas_call(functools.partial(kernel, n, s, groups), out_shape=jax.Sha...  91.2 us
    unnamed x1, local copies, waits for them, and re-layouts  2.46 us

profile of v3, /device:TPU:0, one launch (start us, length us, event | category | flops | bytes accessed | tf_op | source)
XLA Modules:
  0.0 93.7 jit_solution(954569908814177030)
XLA Ops:
  0.0 91.2 %shard_map.64 = bf16[128,5120]{1,0:T(8,128)(2,1)} custom-call(bf16[128,5120]{1,0:T(8,128)(2,1)} %bitcast.7, bf16[128,5120]{1,0:T(8,128)(2,1)} %bitcast.8, bf16[128,2560]{1,0:T(8,128)(2,1)} %bitcast.9, bf16[128,2560]{1,0:T(8,128)(2,1)} %bitcast.10, f32[1,5120]{1,0:T(1,128)} %bitcast.11, f32[2560]{0:T(1024)} %kg_hbm.1), custom_call_target="tpu_custom_call" | custom-call | flops 2684354560 | bytes 5242880 | tf_op jit(solution)/shard_map/pallas_call | solution.py:416
  91.2 2.5 %copy.8 = bf16[1,128,5120]{2,1,0:T(8,128)(2,1)} copy(bf16[1,128,5120]{2,1,0:T(8,128)(2,1)} %bitcast.6) | data formatting | bytes 2621440

commit v4 on v3

--- a/solution.py
+++ b/solution.py
@@ -38,7 +38,7 @@
     bufs = (kbuf, vbuf)
 
     def lot(g):
-        return g // 2
+        return g
 
     partner = jnp.where(r == 0, 1, jnp.where(r == 1, 0, jnp.where(r == n - 1, n - 2, n - 1)))
 
@@ -127,7 +127,7 @@
     is_helper = jnp.logical_or(r == 1, r == n - 2) if lending else r < 0
 
     def lent(g):
-        return lax.rem(jnp.int32(g), 2) == 0
+        return lax.rem(jnp.int32(g), 2) == 1
 
     def goes_left(g):
         return r > jnp.where(lent(g), 1, 0) if lending else has_left
@@ -334,7 +334,7 @@
     for g in range(ahead):
         lend_group(g)
 
-    lead, lag = 1, 2
+    lead, lag = 1, 1
 
     def step(i, carry):
         @pl.when(i + ahead < groups)
@@ -409,7 +409,7 @@
     groups = choose_groups(fl // HD)
     fg = fl // groups
     peers = max(s - 1, 1)
-    lots = groups // 2 + 1
+    lots = groups
     anywhere = pl.BlockSpec(memory_space=pl.ANY)
     flops = 2 * 4 * s * t * n * c * fl
     moved = 2 * (3 * t * d + 2 * c * fl)

time: 93.8 us -> 92.8 us (0.989)
  Pallas kernels: 91.2 us -> 90.2 us
    pallas_call x1, Pallas kernels: 91.2 us -> 90.2 us  [shards(): pl.pallas_call(functools.partial(kernel, n, s, groups), out_shape=jax.Sha...]
where the time goes in v4:
time: 92.8 us; the launch traced here: 92.7 us
  Pallas kernels  90.2 us (97%)
  local copies, waits for them, and re-layouts  2.46 us (3%)
    pallas_call x1, Pallas kernels, shards(): pl.pallas_call(functools.partial(kernel, n, s, groups), out_shape=jax.Sha...  90.2 us
    unnamed x1, local copies, waits for them, and re-layouts  2.46 us

profile of v4, /device:TPU:0, one launch (start us, length us, event | category | flops | bytes accessed | tf_op | source)
XLA Modules:
  0.0 92.7 jit_solution(14568874280731827667)
XLA Ops:
  0.0 90.2 %shard_map.64 = bf16[128,5120]{1,0:T(8,128)(2,1)} custom-call(bf16[128,5120]{1,0:T(8,128)(2,1)} %bitcast.7, bf16[128,5120]{1,0:T(8,128)(2,1)} %bitcast.8, bf16[128,2560]{1,0:T(8,128)(2,1)} %bitcast.9, bf16[128,2560]{1,0:T(8,128)(2,1)} %bitcast.10, f32[1,5120]{1,0:T(1,128)} %bitcast.11, f32[2560]{0:T(1024)} %kg_hbm.1), custom_call_target="tpu_custom_call" | custom-call | flops 2684354560 | bytes 5242880 | tf_op jit(solution)/shard_map/pallas_call | solution.py:416
  90.2 2.5 %copy.8 = bf16[1,128,5120]{2,1,0:T(8,128)(2,1)} copy(bf16[1,128,5120]{2,1,0:T(8,128)(2,1)} %bitcast.6) | data formatting | bytes 2621440
